TPU v7x, 256 devices: a whole 4x4x8 slice. The times are simulated.
256 devices in a mesh: queue: 128 (over y_hi, x, z, core), heads: 2 (over y_lo).
Axes of the slice: x: 4, y: 4 (y_hi: 2, y_lo: 2; y = y_hi * 2 + y_lo), z: 8, core: 2. Of those that a mesh axis runs over, the one named last changes fastest.
Arguments:
- latents: bfloat16 [128, 256, 1536], P('queue', None, 'heads'), may hold values from -6 to 6
- fresh_noise: bfloat16 [2, 256, 1536], P(None, None, 'heads'), may hold values from -6 to 6
- level_index: int32 [128], replicated, may hold values from 0 to 1023, as said below
- window_width: int32 [128], replicated, may hold values from 1 to 2
- w_mod: bfloat16 [256, 3, 1536], P(None, None, 'heads'), may hold values from -0.375 to 0.375
- w_query: bfloat16 [1536, 1536], P(None, 'heads'), may hold values from -1 to 1
- w_key: bfloat16 [1536, 1536], P(None, 'heads'), may hold values from -1 to 1
- w_value: bfloat16 [1536, 1536], P(None, 'heads'), may hold values from -0.15625 to 0.15625
- w_out: bfloat16 [1536, 1536], P('heads'), may hold values from -0.15625 to 0.15625
Outputs:
- queue_out: bfloat16 [128, 256, 1536], P('queue', None, 'heads')
- velocities: bfloat16 [2, 128, 256, 1536], P(None, 'queue', None, 'heads')
Inputs may be any that keep to these rules, and one draw needn't show every extreme that they name: `level_index`: strictly rising along the queue: slot f holds a level in [f * 8, (f + 1) * 8); slot 0 holds 0 and the last slot 1023.
All inputs are finite; a program needn't handle non-finite values.
Results may differ from a plain program's by a relative error of at most 0.008.
Values may be sent and summed in bfloat16 or wider, within the bound.
No kernel may reach another device: no remote copies, remote signals or barrier semaphores. Data moves between devices by JAX's collectives and lax.ppermute only.
A program may use at most 64 MiB of HBM per device.

v0:
```python
import functools
import math

import jax
import jax.numpy as jnp
from jax import lax
from jax.experimental import pallas as pl
from jax.experimental.pallas import tpu as pltpu
from jax.sharding import PartitionSpec as P

HEAD_DIM = 128
STRIDE = 8
NORM_EPS = 1e-06
BF16 = jnp.bfloat16
F32 = jnp.float32
VMEM_LIMIT = 32 * 1024 * 1024
SCORE_FACTOR = math.log2(math.e) / math.sqrt(HEAD_DIM)
SLOTS = 5
SHIFT, SCALE, GATE, CHANGE = 0, SLOTS, 2 * SLOTS, 3 * SLOTS
TABLE_ROWS = 24


def dot(a, b):
    return jnp.dot(a, b, preferred_element_type=F32)


def whole(shape):
    return pl.BlockSpec(shape, functools.partial(lambda n, *_: (0,) * n, len(shape)))


def call(body, meta, args, specs, outs, scratch=(), room=VMEM_LIMIT):
    return pl.pallas_call(
        body,
        grid_spec=pltpu.PrefetchScalarGridSpec(
            num_scalar_prefetch=len(meta),
            grid=(1,),
            in_specs=[whole(a.shape) if s is None else s for a, s in zip(args, specs)],
            out_specs=[whole(o.shape) for o in outs],
            scratch_shapes=scratch,
        ),
        out_shape=outs,
        compiler_params=pltpu.CompilerParams(vmem_limit_bytes=room),
        cost_estimate=pl.CostEstimate(flops=1, bytes_accessed=1, transcendentals=0),
    )(*meta, *args)


def sigma_of(level, levels):
    share = level / levels
    return 5.0 * share / (1.0 + 4.0 * share)


def prepare_body(queue, meta_ref, level_ref, w_mod, mod_ref):
    place, behind = meta_ref[2], meta_ref[3]
    before = (place - 1) & (queue - 1)
    rows = lax.broadcasted_iota(jnp.int32, (16, w_mod.shape[1] // 2), 0)
    level = jnp.zeros(rows.shape, jnp.int32)
    for i, at in enumerate((place, place ^ 2, behind, before, place ^ 1)):
        level = jnp.where(rows == i, level_ref[at], level)
    freqs = w_mod.shape[1] // 2
    index_k = lax.broadcasted_iota(jnp.int32, (16, freqs), 1).astype(F32)
    phase = level.astype(F32) * jnp.exp(-math.log(10000.0) * index_k / freqs)
    low = jnp.cos(phase).astype(BF16)
    high = jnp.sin(phase).astype(BF16)
    for kind in range(3):
        table = dot(low, w_mod[kind, :freqs, :]) + dot(high, w_mod[kind, freqs:, :])
        mod_ref[SLOTS * kind : SLOTS * (kind + 1), :] = table[:SLOTS, :]
    levels = queue * STRIDE
    for i, slot in enumerate((place, before)):
        sigma = [
            sigma_of(jnp.full((1, mod_ref.shape[1]), level_ref[at], jnp.int32).astype(F32), levels)
            for at in (slot, (slot - 1) & (queue - 1))
        ]
        mod_ref[CHANGE + i : CHANGE + i + 1, :] = jnp.where(slot > 0, sigma[1], 0.0) - sigma[0]
    unused = TABLE_ROWS - CHANGE - 2
    mod_ref[CHANGE + 2 :, :] = jnp.zeros((unused, mod_ref.shape[1]), F32)


def pack_body(meta_ref, wq, wk, wv, w_rows, query_ref, pair_ref, wide_ref, narrow_ref):
    group = wk.shape[1]
    query_ref[...] = wq[...]
    pair_ref[:, :group] = wk[...]
    pair_ref[:, group:] = wv[...]
    wide = wide_ref.shape[0]
    wide_ref[...] = w_rows[:wide, :]
    narrow_ref[...] = w_rows[wide:, :]


def lane_block(index, width):
    return pl.ds(pl.multiple_of(index * width, HEAD_DIM), width)


def normalize(a, b, mod_a, mod_b, slot, side, out_ref):
    a = a.astype(F32)
    b = b.astype(F32)
    half = a.shape[1]
    width = 2 * half
    total = jnp.sum(a, axis=-1, keepdims=True) + jnp.sum(b, axis=-1, keepdims=True)
    square = jnp.sum(a * a, axis=-1, keepdims=True) + jnp.sum(b * b, axis=-1, keepdims=True)
    mean = total / width
    inv = lax.rsqrt(square / width - mean * mean + NORM_EPS)
    for x, mod, at in ((a, mod_a, side), (b, mod_b, 1 - side)):
        scale, shift = mod(SCALE + slot), mod(SHIFT + slot)
        out_ref[:, lane_block(at, half)] = (
            (x - mean) * inv * (1.0 + scale) + shift
        ).astype(BF16)


def norm_body(jobs, meta_ref, *refs):
    count = len(jobs)
    mod_m, mod_t = refs[2 * count : 2 * count + 2]
    for i, (slot, may_cross) in enumerate(jobs):
        side = meta_ref[0]
        row_m = lambda r: mod_m[r : r + 1, :]
        row_t = lambda r: mod_t[r : r + 1, :]
        if may_cross:
            crossed = meta_ref[4] == 1
            side = side ^ meta_ref[4]
            mod_a = lambda r: jnp.where(crossed, row_t(r), row_m(r))
            mod_b = lambda r: jnp.where(crossed, row_m(r), row_t(r))
        else:
            mod_a, mod_b = row_m, row_t
        normalize(
            refs[2 * i][...], refs[2 * i + 1][...], mod_a, mod_b, slot, side,
            refs[2 * count + 2 + i],
        )


def lane_max(scores, allowed):
    best = None
    for s, ok in zip(scores, allowed):
        top = s[:, :HEAD_DIM]
        for at in range(HEAD_DIM, s.shape[1], HEAD_DIM):
            top = jnp.maximum(top, s[:, at : at + HEAD_DIM])
        top = jnp.where(ok, top, -1e30)
        best = top if best is None else jnp.maximum(best, top)
    return jnp.max(best, axis=-1, keepdims=True)


def weigh(scores, allowed, top, values):
    total, mixed = None, None
    for s, ok, v in zip(scores, allowed, values):
        w = jnp.exp2(s - jnp.where(ok, top, 1e30))
        part = w[:, :HEAD_DIM]
        for at in range(HEAD_DIM, s.shape[1], HEAD_DIM):
            part = part + w[:, at : at + HEAD_DIM]
        total = part if total is None else total + part
        product = dot(w.astype(BF16), v)
        mixed = product if mixed is None else mixed + product
    return jnp.sum(total, axis=-1, keepdims=True), mixed


def scores_of(query, keys):
    return lax.dot_general(query, keys, (((1,), (1,)), ((), ())), preferred_element_type=F32)


def within(slot, offset, reach, queue):
    at = slot + offset
    return (jnp.abs(offset) <= reach) & (at >= 0) & (at < queue)


def first_local_body(
    queue, meta_ref, width_ref, own_m, own_t, other_m, other_t, mod_m, mod_t, wq, wkv,
    q_ref, acc_ref, stat_ref, kv_ref, normed,
):
    row_m = lambda r: mod_m[r : r + 1, :]
    row_t = lambda r: mod_t[r : r + 1, :]
    side = meta_ref[0]
    normalize(own_m[...], own_t[...], row_m, row_t, 0, side, normed.at[0])
    normalize(other_m[...], other_t[...], row_m, row_t, 4, side, normed.at[1])
    project_body(meta_ref, normed.at[0], normed.at[1], wq, wkv, q_ref, kv_ref)
    local_body(0, queue, meta_ref, width_ref, q_ref, kv_ref, acc_ref, stat_ref)


def project_body(meta_ref, own, other, wq, wkv, q_ref, kv_ref):
    for i, frame in enumerate((own, other)):
        kv_ref[i] = dot(frame[...], wkv[...]).astype(BF16)
        q_ref[i] = (dot(frame[...], wq[...]) * SCORE_FACTOR).astype(BF16)


def local_body(step, queue, meta_ref, width_ref, q_ref, kv_ref, acc_ref, stat_ref):
    place = meta_ref[2]
    group = kv_ref.shape[2] // 2
    for qi in range(2):
        here = place ^ qi
        slot = (here - step) & (queue - 1)
        reach = width_ref[slot]
        aside = 1 - 2 * (here & 1)
        allowed = (reach >= 0, within(slot, aside, reach, queue))
        for head in range(group // HEAD_DIM):
            lanes = slice(head * HEAD_DIM, (head + 1) * HEAD_DIM)
            value_lanes = slice(group + head * HEAD_DIM, group + (head + 1) * HEAD_DIM)
            query = q_ref[qi, :, lanes]
            scores = [scores_of(query, kv_ref[j, :, lanes]) for j in (qi, 1 - qi)]
            top = lane_max(scores, allowed)
            values = [kv_ref[j, :, value_lanes] for j in (qi, 1 - qi)]
            total, mixed = weigh(scores, allowed, top, values)
            acc_ref[qi, :, lanes] = mixed
            stat_ref[qi, :, head : head + 1] = top
            stat_ref[qi, :, 8 + head : 9 + head] = total


def halo_body(
    step, queue, meta_ref, width_ref, *refs
):
    sources, (q_ref, acc_in, stat_in, own_out, other_out, ks, vs) = refs[:-7], refs[-7:]
    group = ks.shape[2]
    place, behind = meta_ref[2], meta_ref[3]
    if step == 0:
        *frames, wkv = sources
        for i, frame in enumerate(frames):
            both = dot(frame[...], wkv[...])
            ks[i] = both[:, :group].astype(BF16)
            vs[i] = both[:, group:].astype(BF16)
    else:
        for i in range(4):
            ks[i] = sources[i // 2][i % 2, :, :group]
            vs[i] = sources[i // 2][i % 2, :, group:]
    for qi, out in enumerate((own_out, other_out)):
        here = place ^ qi
        slot = (here - step) & (queue - 1)
        reach = width_ref[slot]
        index, allowed = [], []
        for offset in (-2, 2, 2 * (here & 1) - 1):
            there = (here + offset) & (queue - 1)
            pick = jnp.int32(3)
            for j, known in enumerate((place ^ 2, place ^ 3, behind)):
                pick = jnp.where(there == known, j, pick)
            index.append(pick)
            allowed.append(within(slot, jnp.int32(offset), reach, queue))
        for head in range(ks.shape[2] // HEAD_DIM):
            lanes = slice(head * HEAD_DIM, (head + 1) * HEAD_DIM)
            query = q_ref[qi, :, lanes]
            scores = [scores_of(query, ks[j, :, lanes]) for j in index]
            before = stat_in[qi, :, head : head + 1]
            top = jnp.maximum(before, lane_max(scores, allowed))
            total, mixed = weigh(scores, allowed, top, [vs[j, :, lanes] for j in index])
            fade = jnp.exp2(before - top)
            total = total + fade * stat_in[qi, :, 8 + head : 9 + head]
            mixed = mixed + fade * acc_in[qi, :, lanes]
            out[:, lanes] = (mixed / total).astype(BF16)


def output_sums(mixed, weights):
    m_self, m_core, m_y, m_yx = mixed
    w_self, w_core, w_y0, w_y1, w_x0, w_x1 = weights
    wide = w_y0.shape[0]
    sums = dot(m_self[...], w_self[...]) + dot(m_core[...], w_core[...])
    sums += dot(m_y[:, :wide], w_y0[...]) + dot(m_y[:, wide:], w_y1[...])
    return sums + dot(m_yx[:, :wide], w_x0[...]) + dot(m_yx[:, wide:], w_x1[...])


def out_step_body(
    meta_ref,
    m_self, m_core, m_y, m_yx, *rest,
):
    lat_m, lat_t, fresh_m, fresh_t, mod_m, mod_t, vel_ref, next_ref, normed_ref = rest[12:]
    mixed = m_self, m_core, m_y, m_yx
    change = mod_m[CHANGE : CHANGE + 1, :]
    first = meta_ref[2] == 0
    fresh = (fresh_m[0], fresh_t[...])
    nexts = []
    for side, (lat, mod) in enumerate(((lat_m, mod_m), (lat_t, mod_t))):
        proj = output_sums(mixed, rest[6 * side : 6 * side + 6])
        state = lat[...].astype(F32)
        velocity = state + mod[GATE : GATE + 1, :] * proj
        updated = (state + change * velocity).astype(BF16)
        if side == 0:
            vel_ref[...] = velocity.astype(BF16)
        nexts.append(jnp.where(first, fresh[side].astype(F32), updated.astype(F32)))
    next_ref[...] = nexts[0].astype(BF16)
    normalize(
        nexts[0], nexts[1], lambda r: mod_m[r : r + 1, :], lambda r: mod_t[r : r + 1, :],
        3, meta_ref[0], normed_ref,
    )


def out_last_body(
    meta_ref,
    m_self, m_core, m_y, m_yx, *rest,
):
    latent, fresh, mod_m, vel_ref, upd_ref = rest[6:]
    proj = output_sums((m_self, m_core, m_y, m_yx), rest[:6])
    state = latent[...].astype(F32)
    velocity = state + mod_m[GATE + 3 : GATE + 4, :] * proj
    vel_ref[...] = velocity.astype(BF16)
    updated = state + mod_m[CHANGE + 1 : CHANGE + 2, :] * velocity
    leaves = meta_ref[2] == 1
    upd_ref[...] = jnp.where(leaves, fresh[0].astype(F32), updated).astype(BF16)


def join_body(meta_ref, latent, first, second, latent_ref, both_ref):
    latent_ref[...] = latent[...]
    both_ref[0] = first[...]
    both_ref[1] = second[...]


def tie(*arrays):
    return lax.optimization_barrier(arrays)


def per_device(
    latents, fresh_noise, level_index, window_width, w_mod, w_query, w_key, w_value, w_out
):
    queue = lax.axis_size("queue")
    place = lax.axis_index("queue")
    side = lax.axis_index("heads")
    core = place & 1
    chips = queue // 2

    def behind_of(f):
        chip = f >> 1
        return (((chip + 1 if chip & 1 else chip - 1) % chips) << 1) | (f & 1)

    chip = place >> 1
    behind = ((jnp.where(chip & 1 == 1, chip + 1, chip - 1) & (chips - 1)) << 1) | core
    crossed = ((place ^ behind) // chips) & 1
    meta = jnp.stack(
        [side, core, place, behind, crossed]
    ).astype(jnp.int32)

    rows, half = latents.shape[1:]
    group = half // 2
    wide = group - HEAD_DIM
    slots = range(queue)

    core_swap = [(f, f ^ 1) for f in slots]
    near = [(f, f ^ 2) for f in slots]
    far_ring = [
        (f * 2 + h, behind_of(f) * 2 + (h ^ (((f ^ behind_of(f)) // chips) & 1)))
        for f in slots
        for h in (0, 1)
    ]
    far_open = [(s, d if abs(s // 2 - d // 2) <= 2 else s) for s, d in far_ring]
    head_only = [(s, s ^ 1 if s < 2 else s) for s in range(2 * queue)]
    both = ("queue", "heads")

    def on_queue(x, perm):
        return lax.ppermute(x, "queue", perm)

    def on_sides(x):
        return lax.ppermute(x, "heads", [(0, 1), (1, 0)])

    def on_both(x, perm):
        return lax.ppermute(x, both, perm)

    def aside(to):
        return [(f * 2 + h, to(f) * 2 + 1 - h) for f in slots for h in (0, 1)]

    frame = jax.ShapeDtypeStruct((rows, 2 * half), BF16)
    half_frame = jax.ShapeDtypeStruct((rows, half), BF16)
    piece = jax.ShapeDtypeStruct((rows, group), BF16)
    pair = jax.ShapeDtypeStruct((2, rows, group), BF16)
    sums = jax.ShapeDtypeStruct((2, rows, group), F32)
    stats = jax.ShapeDtypeStruct((2, rows, HEAD_DIM), F32)

    def columns():
        return pl.BlockSpec((2 * half, group), lambda i, m, *_: (0, m[1]))

    def fresh_spec(step):
        return pl.BlockSpec((1, rows, half), lambda *_: (step, 0, 0))

    mine = latents[0]
    theirs = on_sides(mine)
    near_mine = on_queue(mine, near)
    far_mine = on_both(mine, far_open)

    (mod_mine,) = call(
        functools.partial(prepare_body, queue), [meta, level_index],
        [jnp.transpose(w_mod, (1, 0, 2))], [None],
        [jax.ShapeDtypeStruct((TABLE_ROWS, half), F32)],
    )
    mod_theirs = on_sides(mod_mine)
    w_query, w_pair, *send = call(
        pack_body, [meta], [w_query, w_key, w_value, w_out],
        [columns()] * 3 + [pl.BlockSpec((group, 2 * half), lambda i, m, *_: (m[1], 0))],
        [
            jax.ShapeDtypeStruct((2 * half, n), BF16) for n in (group, 2 * group)
        ] + [
            jax.ShapeDtypeStruct((n, 2 * half), BF16) for n in (wide, group - wide)
        ],
        room=58 * 1024 * 1024,
    )
    other_mine = on_queue(mine, core_swap)
    near_mine, far_mine, theirs, mod_mine, w_query, w_pair = tie(
        near_mine, far_mine, theirs, mod_mine, w_query, w_pair
    )
    other_theirs = on_queue(theirs, core_swap)

    def normed(pairs, jobs):
        args = [x for p in pairs for x in p] + [mod_mine, mod_theirs]
        return call(
            functools.partial(norm_body, jobs), [meta], args, [None] * len(args),
            [frame] * len(pairs),
        )

    def halo(step, sources, state):
        args = sources + state
        return call(
            functools.partial(halo_body, step, queue), [meta, window_width], args,
            [None] * len(args), [piece, piece],
            scratch=[pltpu.VMEM((4, rows, group), BF16)] * 2,
        )

    def exchanged(m_own, m_other):
        return [
            m_own, on_queue(m_other, core_swap), on_sides(m_own),
            on_both(m_other, aside(lambda f: f ^ 1)),
        ]

    def w_specs(flip):
        col = (lambda m: 1 - m[0]) if flip else (lambda m: m[0])
        return [
            pl.BlockSpec((group, half), lambda i, m, *_: (m[1], col(m))),
            pl.BlockSpec((group, half), lambda i, m, *_: (1 - m[1], col(m))),
        ] + [
            pl.BlockSpec((n, half), lambda i, m, *_: (0, col(m))) for n in (wide, group - wide)
        ] * 2

    near_theirs = on_sides(near_mine)
    far_theirs = on_both(theirs, far_open)
    state = call(
        functools.partial(first_local_body, queue), [meta, window_width],
        [mine, theirs, other_mine, other_theirs, mod_mine, mod_theirs, w_query, w_pair],
        [None] * 8, [pair, sums, stats],
        scratch=[
            pltpu.VMEM((2, rows, 2 * group), BF16), pltpu.VMEM((2, rows, 2 * half), BF16)
        ],
    )
    fresh_theirs = on_both(fresh_noise[0], head_only)
    near_theirs, far_theirs, fresh_theirs, *state = tie(
        near_theirs, far_theirs, fresh_theirs, *state
    )
    near_own, far_own = normed(
        [(near_mine, near_theirs), (far_mine, far_theirs)], [(1, False), (2, True)]
    )
    near_own, far_own, *send = tie(near_own, far_own, *send)
    far_weights = [on_both(send[0], aside(lambda f: f ^ chips)), on_sides(send[1])]
    near_own, far_own, *state = tie(near_own, far_own, *state)
    near_other = on_queue(near_own, core_swap)
    far_other = on_queue(far_own, core_swap)
    m_own, m_other = halo(0, [near_own, near_other, far_own, far_other, w_pair], state)
    mixed = exchanged(m_own, m_other)
    *far_weights, _, _ = tie(*far_weights, mixed[2], mixed[3])
    far_weights_other = [on_queue(w, core_swap) for w in far_weights]
    weights = [w_out, w_out, *far_weights, *far_weights_other]
    vel0, latent, own = call(
        out_step_body, [meta],
        mixed + weights * 2
        + [mine, theirs, fresh_noise, fresh_theirs, mod_mine, mod_theirs],
        [None] * 4 + w_specs(False) + w_specs(True) + [None, None, fresh_spec(0), None, None, None],
        [half_frame, half_frame, frame],
    )

    query, keyed = call(
        project_body, [meta], [own, on_queue(own, core_swap), w_query, w_pair], [None] * 4,
        [pair, jax.ShapeDtypeStruct((2, rows, 2 * group), BF16)],
    )
    near_keyed = on_queue(keyed, near)
    far_keyed = on_queue(keyed, [(f, behind_of(f)) for f in slots])
    sums0, stats0 = call(
        functools.partial(local_body, 1, queue), [meta, window_width], [query, keyed],
        [None] * 2, [sums, stats],
    )
    mixed = exchanged(*halo(1, [near_keyed, far_keyed], [query, sums0, stats0]))
    vel1, upd1 = call(
        out_last_body, [meta], mixed + weights + [latent, fresh_noise, mod_mine],
        [None] * 4 + w_specs(False) + [None, fresh_spec(1), None],
        [half_frame, half_frame],
    )
    latent = on_queue(upd1, [(f, (f - 2) % queue) for f in slots])
    vel1 = on_queue(vel1, [(f, (f - 1) % queue) for f in slots])
    latent, velocities = call(
        join_body, [meta], [latent, vel0, vel1], [None] * 3,
        [half_frame, jax.ShapeDtypeStruct((2, rows, half), BF16)],
    )
    return (latent[None], velocities[:, None])


def solution(mesh):
    in_specs = (
        P("queue", None, "heads"),
        P(None, None, "heads"),
        P(),
        P(),
        P(None, None, "heads"),
        P(None, "heads"),
        P(None, "heads"),
        P(None, "heads"),
        P("heads", None),
    )
    out_specs = (P("queue", None, "heads"), P(None, "queue", None, "heads"))
    return jax.shard_map(
        per_device, mesh=mesh, in_specs=in_specs, out_specs=out_specs, check_vma=False
    )
```

profile of v0, /device:TPU:231, one launch (start us, length us, event | category | flops | bytes accessed | tf_op | source)
XLA Modules:
  0.0 137.9 jit_solution(4102618790026500691)
XLA Ops:
  0.6 1.4 %collective-permute-start.2 = (bf16[256,768]{1,0:T(8,128)(2,1)}, bf16[256,768]{1,0:T(8,128)(2,1)S(1)}, u32[]{:S(2)}, u32[]{:S(2)}) collective-permute-start(bf16[256,768]{1,0:T(8,128)(2,1)} %bitcast.13), channel_id=1, source_target_pairs={{0,1},{1,0},{2,3},{3,2},{4,5},{5,4},{6,7},{7,6},{8,9},{9,8},{10,11... | collective-permute-start | bytes 1179656 | tf_op jit(solution)/shard_map/ppermute | solution.py:341
  2.0 1.9 %collective-permute-start.1 = (bf16[256,768]{1,0:T(8,128)(2,1)}, bf16[256,768]{1,0:T(8,128)(2,1)S(1)}, u32[]{:S(2)}, u32[]{:S(2)}) collective-permute-start(bf16[256,768]{1,0:T(8,128)(2,1)} %bitcast.14), channel_id=1, source_target_pairs={{0,0},{1,1},{2,2},{3,3},{4,8},{5,9},{6,10},{7,11},{8,4},{9,5},{10,... | collective-permute-start | bytes 1179656 | tf_op jit(solution)/shard_map/ppermute | solution.py:344
  3.9 1.5 %collective-permute-start = (bf16[256,768]{1,0:T(8,128)(2,1)}, bf16[256,768]{1,0:T(8,128)(2,1)S(1)}, u32[]{:S(2)}, u32[]{:S(2)}) collective-permute-start(bf16[256,768]{1,0:T(8,128)(2,1)} %bitcast.15), channel_id=1, source_target_pairs={{0,4},{2,6},{4,0},{6,2},{8,12},{10,14},{12,8},{14,10},{16,20},{18,... | collective-permute-start | bytes 1179656 | tf_op jit(solution)/shard_map/ppermute | solution.py:338
  5.5 1.5 %collective-permute-start.6 = (bf16[256,768]{1,0:T(8,128)(2,1)}, bf16[256,768]{1,0:T(8,128)(2,1)S(1)}, u32[]{:S(2)}, u32[]{:S(2)}) collective-permute-start(bf16[256,768]{1,0:T(8,128)(2,1)} %bitcast.16), channel_id=1, source_target_pairs={{0,2},{2,0},{4,6},{6,4},{8,10},{10,8},{12,14},{14,12},{16,18},{18,... | collective-permute-start | bytes 1179656 | tf_op jit(solution)/shard_map/ppermute | solution.py:338
  7.1 1.3 copy-done.7
  10.1 5.6 %shard_map.105 = (bf16[1536,384]{1,0:T(8,128)(2,1)}, bf16[1536,768]{1,0:T(8,128)(2,1)}, bf16[256,1536]{1,0:T(8,128)(2,1)}, bf16[128,1536]{1,0:T(8,128)(2,1)}) custom-call(s32[5]{0:T(128)} %copy-done.8, bf16[1536,768]{1,0:T(8,128)(2,1)} %wq.1, bf16[1536,768]{1,0:T(8,128)(2,1)} %wk.1, bf16[1536,768]{1,0:T(8,128)(2,1)} %wv.1, bf16[768,1536]{1,0:T(8,128)(2,1)} %rest_1_.3), custom_call_target="tpu_custom_call" | custom-call | flops 1 | bytes 1 | tf_op jit(solution)/shard_map/pallas_call | solution.py:32
  15.7 3.5 %collective-permute-done.1.refs_2_ = bf16[256,768]{1,0:T(8,128)(2,1)S(1)} collective-permute-done((bf16[256,768]{1,0:T(8,128)(2,1)}, bf16[256,768]{1,0:T(8,128)(2,1)S(1)}, u32[]{:S(2)}, u32[]{:S(2)}) %collective-permute-start.1) | collective-permute-done | bytes 393248 | tf_op jit(solution)/shard_map/ppermute | solution.py:344
  19.2 1.9 %collective-permute-start.7 = (bf16[256,768]{1,0:T(8,128)(2,1)S(1)}, bf16[256,768]{1,0:T(8,128)(2,1)S(1)}, u32[]{:S(2)}, u32[]{:S(2)}) collective-permute-start(bf16[256,768]{1,0:T(8,128)(2,1)S(1)} %collective-permute-done.2.own_t.rest_13_), channel_id=1, source_target_pairs={{0,2},{2,0},{4,6},{6,4},{8,10},{10,8},{12,14},{14,12},{16,18},{18,... | collective-permute-start | bytes 1179656 | tf_op jit(solution)/shard_map/ppermute | solution.py:338
  22.0 3.5 %collective-permute-start.4 = (bf16[256,768]{1,0:T(8,128)(2,1)S(1)}, bf16[256,768]{1,0:T(8,128)(2,1)S(1)}, u32[]{:S(2)}, u32[]{:S(2)}) collective-permute-start(bf16[256,768]{1,0:T(8,128)(2,1)S(1)} %collective-permute-done.2.own_t.rest_13_), channel_id=1, source_target_pairs={{0,0},{1,1},{2,2},{3,3},{4,8},{5,9},{6,10},{7,11},{8,4},{9,5},{10,... | collective-permute-start | bytes 1179656 | tf_op jit(solution)/shard_map/ppermute | solution.py:344
  25.6 1.7 %copy-done.1 = bf16[1536,768]{1,0:T(8,128)(2,1)S(1)} copy-done((bf16[1536,768]{1,0:T(8,128)(2,1)S(1)}, bf16[1536,768]{1,0:T(8,128)(2,1)}, u32[]{:S(2)}) %copy-start.1) | copy-done | bytes 2359320
  27.2 1.3 copy-done.4
  29.1 5.9 %shard_map.106 = (bf16[2,256,384]{2,1,0:T(8,128)(2,1)S(1)}, f32[2,256,384]{2,1,0:T(8,128)S(1)}, f32[2,256,128]{2,1,0:T(8,128)S(1)}) custom-call(s32[5]{0:T(128)S(1)} %copy-done.9, s32[128]{0:T(128)S(1)} %copy-done.10, bf16[256,768]{1,0:T(8,128)(2,1)S(1)} %bitcast.17, bf16[256,768]{1,0:T(8,128)(2,1)S(1)} %collective-permute-done.2.own_t.rest_13_, ...), custom_call_target="tpu_custom_call" | custom-call | flops 1 | bytes 1 | tf_op jit(solution)/shard_map/pallas_call | solution.py:32
  35.0 5.1 %collective-permute-done.4.refs_3_ = bf16[256,768]{1,0:T(8,128)(2,1)S(1)} collective-permute-done((bf16[256,768]{1,0:T(8,128)(2,1)S(1)}, bf16[256,768]{1,0:T(8,128)(2,1)S(1)}, u32[]{:S(2)}, u32[]{:S(2)}) %collective-permute-start.4) | collective-permute-done | bytes 393248 | tf_op jit(solution)/shard_map/ppermute | solution.py:344
  40.1 1.7 %shard_map.107 = (bf16[256,1536]{1,0:T(8,128)(2,1)S(1)}, bf16[256,1536]{1,0:T(8,128)(2,1)S(1)}) custom-call(s32[5]{0:T(128)S(1)} %copy-done.9, bf16[256,768]{1,0:T(8,128)(2,1)S(1)} %collective-permute-done.refs_0_, bf16[256,768]{1,0:T(8,128)(2,1)S(1)} %collective-permute-done.3.refs_1_, bf16[256,768]{1,0:T(8,128)(2,1)S(1)} %collective-permute-done.1.refs_2_, ...), custom_call_target="tpu_custom_call" | custom-call | flops 1 | bytes 1 | tf_op jit(solution)/shard_map/pallas_call | solution.py:32
  43.3 1.3 collective-permute-done.9.refs_1_
  45.7 6.0 %shard_map.108 = (bf16[256,384]{1,0:T(8,128)(2,1)S(1)}, bf16[256,384]{1,0:T(8,128)(2,1)S(1)}) custom-call(s32[5]{0:T(128)S(1)} %copy-done.9, s32[128]{0:T(128)S(1)} %copy-done.10, bf16[256,1536]{1,0:T(8,128)(2,1)S(1)} %get-tuple-element.71.refs_0_, bf16[256,1536]{1,0:T(8,128)(2,1)S(1)} %collective-permute-done.9.refs_1_, ...), custom_call_target="tpu_custom_call" | custom-call | flops 1 | bytes 1 | tf_op jit(solution)/shard_map/pallas_call | solution.py:32
  52.1 1.8 %collective-permute-start.13 = (bf16[256,384]{1,0:T(8,128)(2,1)S(1)}, bf16[256,384]{1,0:T(8,128)(2,1)S(1)}, u32[]{:S(2)}, u32[]{:S(2)}) collective-permute-start(bf16[256,384]{1,0:T(8,128)(2,1)S(1)} %get-tuple-element.77), channel_id=1, source_target_pairs={{0,3},{1,2},{2,1},{3,0},{4,7},{5,6},{6,5},{7,4},{8,11},{9,10},{10,... | collective-permute-start | bytes 589832 | tf_op jit(solution)/shard_map/ppermute | solution.py:344
  53.8 8.8 %collective-permute-done.14.rest_2_.rest_8_ = bf16[256,1536]{1,0:T(8,128)(2,1)S(1)} collective-permute-done((bf16[256,1536]{1,0:T(8,128)(2,1)S(1)}, bf16[256,1536]{1,0:T(8,128)(2,1)S(1)}, u32[]{:S(2)}, u32[]{:S(2)}) %collective-permute-start.14) | collective-permute-done | bytes 786464 | tf_op jit(solution)/shard_map/ppermute | solution.py:344
  64.4 2.2 %collective-permute-done.11.m_core = bf16[256,384]{1,0:T(8,128)(2,1)S(1)} collective-permute-done((bf16[256,384]{1,0:T(8,128)(2,1)S(1)}, bf16[256,384]{1,0:T(8,128)(2,1)S(1)}, u32[]{:S(2)}, u32[]{:S(2)}) %collective-permute-start.11) | collective-permute-done | bytes 196640 | tf_op jit(solution)/shard_map/ppermute | solution.py:338
  66.7 3.1 %shard_map.109 = (bf16[256,768]{1,0:T(8,128)(2,1)S(1)}, bf16[256,768]{1,0:T(8,128)(2,1)S(1)}, bf16[256,1536]{1,0:T(8,128)(2,1)S(1)}) custom-call(s32[5]{0:T(128)S(1)} %copy-done.9, bf16[256,384]{1,0:T(8,128)(2,1)S(1)} %get-tuple-element.76.m_self, bf16[256,384]{1,0:T(8,128)(2,1)S(1)} %collective-permute-done.11.m_core, ...), custom_call_target="tpu_custom_call" | custom-call | flops 1 | bytes 1 | tf_op jit(solution)/shard_map/pallas_call | solution.py:32
  70.2 1.9 %collective-permute-done.18.other = bf16[256,1536]{1,0:T(8,128)(2,1)S(1)} collective-permute-done((bf16[256,1536]{1,0:T(8,128)(2,1)S(1)}, bf16[256,1536]{1,0:T(8,128)(2,1)S(1)}, u32[]{:S(2)}, u32[]{:S(2)}) %collective-permute-start.18) | collective-permute-done | bytes 786464 | tf_op jit(solution)/shard_map/ppermute | solution.py:338
  72.1 2.7 %shard_map.110 = (bf16[2,256,384]{2,1,0:T(8,128)(2,1)S(1)}, bf16[2,256,768]{2,1,0:T(8,128)(2,1)S(1)}) custom-call(s32[5]{0:T(128)S(1)} %copy-done.9, bf16[256,1536]{1,0:T(8,128)(2,1)S(1)} %get-tuple-element.83.own, bf16[256,1536]{1,0:T(8,128)(2,1)S(1)} %collective-permute-done.18.other, bf16[1536,384]{1,0:T(8,128)(2,1)S(1)} %copy-done.5, ...), custom_call_target="tpu_custom_call" | custom-call | flops 1 | bytes 1 | tf_op jit(solution)/shard_map/pallas_call | solution.py:32
  75.8 2.5 %shard_map.111 = (f32[2,256,384]{2,1,0:T(8,128)S(1)}, f32[2,256,128]{2,1,0:T(8,128)S(1)}) custom-call(s32[5]{0:T(128)S(1)} %copy-done.9, s32[128]{0:T(128)S(1)} %copy-done.10, bf16[2,256,384]{2,1,0:T(8,128)(2,1)S(1)} %get-tuple-element.85.q_ref.refs_2_, bf16[2,256,768]{2,1,0:T(8,128)(2,1)S(1)} %get-tuple-element.84.kv_ref), custom_call_target="tpu_custom_call" | custom-call | flops 1 | bytes 1 | tf_op jit(solution)/shard_map/pallas_call | solution.py:32
  78.4 21.3 %collective-permute-done.20.refs_1_ = bf16[2,256,768]{2,1,0:T(8,128)(2,1)S(1)} collective-permute-done((bf16[2,256,768]{2,1,0:T(8,128)(2,1)S(1)}, bf16[2,256,768]{2,1,0:T(8,128)(2,1)S(1)}, u32[]{:S(2)}, u32[]{:S(2)}) %collective-permute-start.20) | collective-permute-done | bytes 786464 | tf_op jit(solution)/shard_map/ppermute | solution.py:338
  99.7 3.7 %shard_map.112 = (bf16[256,384]{1,0:T(8,128)(2,1)S(1)}, bf16[256,384]{1,0:T(8,128)(2,1)S(1)}) custom-call(s32[5]{0:T(128)S(1)} %copy-done.9, s32[128]{0:T(128)S(1)} %copy-done.10, bf16[2,256,768]{2,1,0:T(8,128)(2,1)S(1)} %collective-permute-done.19.refs_0_, bf16[2,256,768]{2,1,0:T(8,128)(2,1)S(1)} %collective-permute-done.20.refs_1_, ...), custom_call_target="tpu_custom_call" | custom-call | flops 1 | bytes 1 | tf_op jit(solution)/shard_map/pallas_call | solution.py:32
  103.5 2.8 %collective-permute-start.23 = (bf16[256,384]{1,0:T(8,128)(2,1)S(1)}, bf16[256,384]{1,0:T(8,128)(2,1)S(1)}, u32[]{:S(2)}, u32[]{:S(2)}) collective-permute-start(bf16[256,384]{1,0:T(8,128)(2,1)S(1)} %get-tuple-element.89), channel_id=1, source_target_pairs={{0,3},{1,2},{2,1},{3,0},{4,7},{5,6},{6,5},{7,4},{8,11},{9,10},{10,... | collective-permute-start | bytes 589832 | tf_op jit(solution)/shard_map/ppermute | solution.py:344
  106.3 2.3 %collective-permute-done.22.m_y = bf16[256,384]{1,0:T(8,128)(2,1)S(1)} collective-permute-done((bf16[256,384]{1,0:T(8,128)(2,1)S(1)}, bf16[256,384]{1,0:T(8,128)(2,1)S(1)}, u32[]{:S(2)}, u32[]{:S(2)}) %collective-permute-start.22) | collective-permute-done | bytes 196640 | tf_op jit(solution)/shard_map/ppermute | solution.py:341
  108.7 5.7 %collective-permute-done.23.m_yx = bf16[256,384]{1,0:T(8,128)(2,1)S(1)} collective-permute-done((bf16[256,384]{1,0:T(8,128)(2,1)S(1)}, bf16[256,384]{1,0:T(8,128)(2,1)S(1)}, u32[]{:S(2)}, u32[]{:S(2)}) %collective-permute-start.23) | collective-permute-done | bytes 196640 | tf_op jit(solution)/shard_map/ppermute | solution.py:344
  114.3 1.6 %shard_map.113 = (bf16[256,768]{1,0:T(8,128)(2,1)S(1)}, bf16[256,768]{1,0:T(8,128)(2,1)S(1)}) custom-call(s32[5]{0:T(128)S(1)} %copy-done.9, bf16[256,384]{1,0:T(8,128)(2,1)S(1)} %get-tuple-element.88.m_self, bf16[256,384]{1,0:T(8,128)(2,1)S(1)} %collective-permute-done.21.m_core, bf16[256,384]{1,0:T(8,128)(2,1)S(1)} %collective-permute-done.22.m_y, ...), custom_call_target="tpu_custom_call" | custom-call | flops 1 | bytes 1 | tf_op jit(solution)/shard_map/pallas_call | solution.py:32
  116.1 16.4 %collective-permute-done.24.latent = bf16[256,768]{1,0:T(8,128)(2,1)S(1)} collective-permute-done((bf16[256,768]{1,0:T(8,128)(2,1)S(1)}, bf16[256,768]{1,0:T(8,128)(2,1)S(1)}, u32[]{:S(2)}, u32[]{:S(2)}) %collective-permute-start.24) | collective-permute-done | bytes 393248 | tf_op jit(solution)/shard_map/ppermute | solution.py:338
  132.5 3.7 %collective-permute-done.25.second = bf16[256,768]{1,0:T(8,128)(2,1)S(1)} collective-permute-done((bf16[256,768]{1,0:T(8,128)(2,1)S(1)}, bf16[256,768]{1,0:T(8,128)(2,1)S(1)}, u32[]{:S(2)}, u32[]{:S(2)}) %collective-permute-start.25) | collective-permute-done | bytes 393248 | tf_op jit(solution)/shard_map/ppermute | solution.py:338
  136.2 1.6 %shard_map.114 = (bf16[256,768]{1,0:T(8,128)(2,1)}, bf16[2,256,768]{2,1,0:T(8,128)(2,1)}) custom-call(s32[5]{0:T(128)S(1)} %copy-done.9, bf16[256,768]{1,0:T(8,128)(2,1)S(1)} %collective-permute-done.24.latent, bf16[256,768]{1,0:T(8,128)(2,1)S(1)} %get-tuple-element.92.first, bf16[256,768]{1,0:T(8,128)(2,1)S(1)} %collective-permute-done.25.second), custom_call_target="tpu_custom_call" | custom-call | flops 1 | bytes 1 | tf_op jit(solution)/shard_map/pallas_call | solution.py:32
  (61 shorter events, 9.8 us)
Async XLA Ops:
  0.6 15.1 %collective-permute-start.2 = (bf16[256,768]{1,0:T(8,128)(2,1)}, bf16[256,768]{1,0:T(8,128)(2,1)S(1)}, u32[]{:S(2)}, u32[]{:S(2)}) collective-permute-start(bf16[256,768]{1,0:T(8,128)(2,1)} %bitcast.13), channel_id=1, source_target_pairs={{0,1},{1,0},{2,3},{3,2},{4,5},{5,4},{6,7},{7,6},{8,9},{9,8},{10,11... | collective-permute-start | bytes 1179656 | tf_op jit(solution)/shard_map/ppermute | solution.py:341
  2.0 17.2 %collective-permute-start.1 = (bf16[256,768]{1,0:T(8,128)(2,1)}, bf16[256,768]{1,0:T(8,128)(2,1)S(1)}, u32[]{:S(2)}, u32[]{:S(2)}) collective-permute-start(bf16[256,768]{1,0:T(8,128)(2,1)} %bitcast.14), channel_id=1, source_target_pairs={{0,0},{1,1},{2,2},{3,3},{4,8},{5,9},{6,10},{7,11},{8,4},{9,5},{10,... | collective-permute-start | bytes 1179656 | tf_op jit(solution)/shard_map/ppermute | solution.py:344
  3.9 15.3 %collective-permute-start = (bf16[256,768]{1,0:T(8,128)(2,1)}, bf16[256,768]{1,0:T(8,128)(2,1)S(1)}, u32[]{:S(2)}, u32[]{:S(2)}) collective-permute-start(bf16[256,768]{1,0:T(8,128)(2,1)} %bitcast.15), channel_id=1, source_target_pairs={{0,4},{2,6},{4,0},{6,2},{8,12},{10,14},{12,8},{14,10},{16,20},{18,... | collective-permute-start | bytes 1179656 | tf_op jit(solution)/shard_map/ppermute | solution.py:338
  5.5 20.1 %collective-permute-start.6 = (bf16[256,768]{1,0:T(8,128)(2,1)}, bf16[256,768]{1,0:T(8,128)(2,1)S(1)}, u32[]{:S(2)}, u32[]{:S(2)}) collective-permute-start(bf16[256,768]{1,0:T(8,128)(2,1)} %bitcast.16), channel_id=1, source_target_pairs={{0,2},{2,0},{4,6},{6,4},{8,10},{10,8},{12,14},{14,12},{16,18},{18,... | collective-permute-start | bytes 1179656 | tf_op jit(solution)/shard_map/ppermute | solution.py:338
  9.8 15.7 %copy-start.6 = (bf16[1,256,768]{2,1,0:T(8,128)(2,1)S(1)}, bf16[1,256,768]{2,1,0:T(8,128)(2,1)}, u32[]{:S(2)}) copy-start(bf16[1,256,768]{2,1,0:T(8,128)(2,1)} %param.9) | copy-start | bytes 1179652
  9.8 15.7 %copy-start.10 = (s32[128]{0:T(128)S(1)}, s32[128]{0:T(128)}, u32[]{:S(2)}) copy-start(s32[128]{0:T(128)} %width_ref.7) | copy-start | bytes 1540
  9.8 12.2 %collective-permute-start.8 = (f32[24,768]{1,0:T(8,128)S(1)}, f32[24,768]{1,0:T(8,128)S(1)}, u32[]{:S(2)}, u32[]{:S(2)}) collective-permute-start(f32[24,768]{1,0:T(8,128)S(1)} %shard_map.104.mod_m.refs_4_.rest_16_.rest_8_), channel_id=1, source_target_pairs={{0,1},{1,0},{2,3},{3,2},{4,5},{5,4},{6,7},{7,6},{8,9},{9,8},{10,11... | collective-permute-start | bytes 221192 | tf_op jit(solution)/shard_map/ppermute | solution.py:341
  19.2 6.3 %collective-permute-start.7 = (bf16[256,768]{1,0:T(8,128)(2,1)S(1)}, bf16[256,768]{1,0:T(8,128)(2,1)S(1)}, u32[]{:S(2)}, u32[]{:S(2)}) collective-permute-start(bf16[256,768]{1,0:T(8,128)(2,1)S(1)} %collective-permute-done.2.own_t.rest_13_), channel_id=1, source_target_pairs={{0,2},{2,0},{4,6},{6,4},{8,10},{10,8},{12,14},{14,12},{16,18},{18,... | collective-permute-start | bytes 1179656 | tf_op jit(solution)/shard_map/ppermute | solution.py:338
  21.1 21.7 %copy-start.12 = (bf16[256,1536]{1,0:T(8,128)(2,1)S(1)}, bf16[256,1536]{1,0:T(8,128)(2,1)}, u32[]{:S(2)}) copy-start(bf16[256,1536]{1,0:T(8,128)(2,1)} %get-tuple-element.78) | copy-start | bytes 2359300
  21.1 13.9 %collective-permute-start.5 = (bf16[256,768]{1,0:T(8,128)(2,1)S(1)}, bf16[256,768]{1,0:T(8,128)(2,1)S(1)}, u32[]{:S(2)}, u32[]{:S(2)}) collective-permute-start(bf16[256,768]{1,0:T(8,128)(2,1)S(1)} %slice_bitcast_fusion), channel_id=1, source_target_pairs={{0,1},{1,0},{2,2},{3,3},{4,4},{5,5},{6,6},{7,7},{8,8},{9,9},{10,10... | collective-permute-start | bytes 1179656 | tf_op jit(solution)/shard_map/ppermute | solution.py:344
  21.9 13.1 %collective-permute-start.3 = (bf16[256,768]{1,0:T(8,128)(2,1)S(1)}, bf16[256,768]{1,0:T(8,128)(2,1)S(1)}, u32[]{:S(2)}, u32[]{:S(2)}) collective-permute-start(bf16[256,768]{1,0:T(8,128)(2,1)S(1)} %collective-permute-done.refs_0_), channel_id=1, source_target_pairs={{0,1},{1,0},{2,3},{3,2},{4,5},{5,4},{6,7},{7,6},{8,9},{9,8},{10,11... | collective-permute-start | bytes 1179656 | tf_op jit(solution)/shard_map/ppermute | solution.py:341
  22.0 18.1 %collective-permute-start.4 = (bf16[256,768]{1,0:T(8,128)(2,1)S(1)}, bf16[256,768]{1,0:T(8,128)(2,1)S(1)}, u32[]{:S(2)}, u32[]{:S(2)}) collective-permute-start(bf16[256,768]{1,0:T(8,128)(2,1)S(1)} %collective-permute-done.2.own_t.rest_13_), channel_id=1, source_target_pairs={{0,0},{1,1},{2,2},{3,3},{4,8},{5,9},{6,10},{7,11},{8,4},{9,5},{10,... | collective-permute-start | bytes 1179656 | tf_op jit(solution)/shard_map/ppermute | solution.py:344
  29.1 16.6 %copy-start.2 = (bf16[1536,768]{1,0:T(8,128)(2,1)S(1)}, bf16[1536,768]{1,0:T(8,128)(2,1)}, u32[]{:S(2)}) copy-start(bf16[1536,768]{1,0:T(8,128)(2,1)} %get-tuple-element.55.wkv.refs_4_) | copy-start | bytes 7077892
  41.7 24.9 %copy-start = (bf16[768,1536]{1,0:T(8,128)(2,1)S(1)}, bf16[768,1536]{1,0:T(8,128)(2,1)}, u32[]{:S(2)}) copy-start(bf16[768,1536]{1,0:T(8,128)(2,1)} %rest_1_.3) | copy-start | bytes 7077892
  41.8 2.8 %collective-permute-start.9 = (bf16[256,1536]{1,0:T(8,128)(2,1)S(1)}, bf16[256,1536]{1,0:T(8,128)(2,1)S(1)}, u32[]{:S(2)}, u32[]{:S(2)}) collective-permute-start(bf16[256,1536]{1,0:T(8,128)(2,1)S(1)} %get-tuple-element.71.refs_0_), channel_id=1, source_target_pairs={{0,2},{2,0},{4,6},{6,4},{8,10},{10,8},{12,14},{14,12},{16,18},{18,... | collective-permute-start | bytes 2359304 | tf_op jit(solution)/shard_map/ppermute | solution.py:338
  42.6 3.0 %collective-permute-start.10 = (bf16[256,1536]{1,0:T(8,128)(2,1)S(1)}, bf16[256,1536]{1,0:T(8,128)(2,1)S(1)}, u32[]{:S(2)}, u32[]{:S(2)}) collective-permute-start(bf16[256,1536]{1,0:T(8,128)(2,1)S(1)} %get-tuple-element.72.refs_2_), channel_id=1, source_target_pairs={{0,2},{2,0},{4,6},{6,4},{8,10},{10,8},{12,14},{14,12},{16,18},{18,... | collective-permute-start | bytes 2359304 | tf_op jit(solution)/shard_map/ppermute | solution.py:338
  42.8 19.9 %collective-permute-start.14 = (bf16[256,1536]{1,0:T(8,128)(2,1)S(1)}, bf16[256,1536]{1,0:T(8,128)(2,1)S(1)}, u32[]{:S(2)}, u32[]{:S(2)}) collective-permute-start(bf16[256,1536]{1,0:T(8,128)(2,1)S(1)} %copy-done.12), channel_id=1, source_target_pairs={{0,129},{1,128},{2,131},{3,130},{4,133},{5,132},{6,135},{7,134},{8... | collective-permute-start | bytes 2359304 | tf_op jit(solution)/shard_map/ppermute | solution.py:344
  42.8 11.1 %collective-permute-start.15 = (bf16[128,1536]{1,0:T(8,128)(2,1)S(1)}, bf16[128,1536]{1,0:T(8,128)(2,1)S(1)}, u32[]{:S(2)}, u32[]{:S(2)}) collective-permute-start(bf16[128,1536]{1,0:T(8,128)(2,1)S(1)} %copy-done.13), channel_id=1, source_target_pairs={{0,1},{1,0},{2,3},{3,2},{4,5},{5,4},{6,7},{7,6},{8,9},{9,8},{10,11... | collective-permute-start | bytes 1179656 | tf_op jit(solution)/shard_map/ppermute | solution.py:341
  51.7 10.9 %collective-permute-start.12 = (bf16[256,384]{1,0:T(8,128)(2,1)S(1)}, bf16[256,384]{1,0:T(8,128)(2,1)S(1)}, u32[]{:S(2)}, u32[]{:S(2)}) collective-permute-start(bf16[256,384]{1,0:T(8,128)(2,1)S(1)} %get-tuple-element.76.m_self), channel_id=1, source_target_pairs={{0,1},{1,0},{2,3},{3,2},{4,5},{5,4},{6,7},{7,6},{8,9},{9,8},{10,11... | collective-permute-start | bytes 589832 | tf_op jit(solution)/shard_map/ppermute | solution.py:341
  52.1 20.1 %copy-start.5 = (bf16[1536,384]{1,0:T(8,128)(2,1)S(1)}, bf16[1536,384]{1,0:T(8,128)(2,1)}, u32[]{:S(2)}) copy-start(bf16[1536,384]{1,0:T(8,128)(2,1)} %get-tuple-element.54.wq) | copy-start | bytes 3538948
  52.1 10.9 %collective-permute-start.13 = (bf16[256,384]{1,0:T(8,128)(2,1)S(1)}, bf16[256,384]{1,0:T(8,128)(2,1)S(1)}, u32[]{:S(2)}, u32[]{:S(2)}) collective-permute-start(bf16[256,384]{1,0:T(8,128)(2,1)S(1)} %get-tuple-element.77), channel_id=1, source_target_pairs={{0,3},{1,2},{2,1},{3,0},{4,7},{5,6},{6,5},{7,4},{8,11},{9,10},{10,... | collective-permute-start | bytes 589832 | tf_op jit(solution)/shard_map/ppermute | solution.py:344
  63.0 3.7 %collective-permute-start.16 = (bf16[256,1536]{1,0:T(8,128)(2,1)S(1)}, bf16[256,1536]{1,0:T(8,128)(2,1)S(1)}, u32[]{:S(2)}, u32[]{:S(2)}) collective-permute-start(bf16[256,1536]{1,0:T(8,128)(2,1)S(1)} %collective-permute-done.14.rest_2_.rest_8_), channel_id=1, source_target_pairs={{0,2},{2,0},{4,6},{6,4},{8,10},{10,8},{12,14},{14,12},{16,18},{18,... | collective-permute-start | bytes 2359304 | tf_op jit(solution)/shard_map/ppermute | solution.py:338
  63.9 2.8 %collective-permute-start.17 = (bf16[128,1536]{1,0:T(8,128)(2,1)S(1)}, bf16[128,1536]{1,0:T(8,128)(2,1)S(1)}, u32[]{:S(2)}, u32[]{:S(2)}) collective-permute-start(bf16[128,1536]{1,0:T(8,128)(2,1)S(1)} %collective-permute-done.15.rest_3_.rest_9_), channel_id=1, source_target_pairs={{0,2},{2,0},{4,6},{6,4},{8,10},{10,8},{12,14},{14,12},{16,18},{18,... | collective-permute-start | bytes 1179656 | tf_op jit(solution)/shard_map/ppermute | solution.py:338
  64.0 2.7 %collective-permute-start.11 = (bf16[256,384]{1,0:T(8,128)(2,1)S(1)}, bf16[256,384]{1,0:T(8,128)(2,1)S(1)}, u32[]{:S(2)}, u32[]{:S(2)}) collective-permute-start(bf16[256,384]{1,0:T(8,128)(2,1)S(1)} %get-tuple-element.77), channel_id=1, source_target_pairs={{0,2},{2,0},{4,6},{6,4},{8,10},{10,8},{12,14},{14,12},{16,18},{18,... | collective-permute-start | bytes 589832 | tf_op jit(solution)/shard_map/ppermute | solution.py:338
  69.8 2.4 %collective-permute-start.18 = (bf16[256,1536]{1,0:T(8,128)(2,1)S(1)}, bf16[256,1536]{1,0:T(8,128)(2,1)S(1)}, u32[]{:S(2)}, u32[]{:S(2)}) collective-permute-start(bf16[256,1536]{1,0:T(8,128)(2,1)S(1)} %get-tuple-element.83.own), channel_id=1, source_target_pairs={{0,2},{2,0},{4,6},{6,4},{8,10},{10,8},{12,14},{14,12},{16,18},{18,... | collective-permute-start | bytes 2359304 | tf_op jit(solution)/shard_map/ppermute | solution.py:338
  74.9 24.8 %collective-permute-start.20 = (bf16[2,256,768]{2,1,0:T(8,128)(2,1)S(1)}, bf16[2,256,768]{2,1,0:T(8,128)(2,1)S(1)}, u32[]{:S(2)}, u32[]{:S(2)}) collective-permute-start(bf16[2,256,768]{2,1,0:T(8,128)(2,1)S(1)} %get-tuple-element.84.kv_ref), channel_id=1, source_target_pairs={{0,252},{2,254},{4,8},{6,10},{8,4},{10,6},{12,16},{14,18},{16,12},... | collective-permute-start | bytes 2359304 | tf_op jit(solution)/shard_map/ppermute | solution.py:338
  75.8 23.9 %collective-permute-start.19 = (bf16[2,256,768]{2,1,0:T(8,128)(2,1)S(1)}, bf16[2,256,768]{2,1,0:T(8,128)(2,1)S(1)}, u32[]{:S(2)}, u32[]{:S(2)}) collective-permute-start(bf16[2,256,768]{2,1,0:T(8,128)(2,1)S(1)} %get-tuple-element.84.kv_ref), channel_id=1, source_target_pairs={{0,4},{2,6},{4,0},{6,2},{8,12},{10,14},{12,8},{14,10},{16,20},{18,... | collective-permute-start | bytes 2359304 | tf_op jit(solution)/shard_map/ppermute | solution.py:338
  103.4 5.3 %collective-permute-start.22 = (bf16[256,384]{1,0:T(8,128)(2,1)S(1)}, bf16[256,384]{1,0:T(8,128)(2,1)S(1)}, u32[]{:S(2)}, u32[]{:S(2)}) collective-permute-start(bf16[256,384]{1,0:T(8,128)(2,1)S(1)} %get-tuple-element.88.m_self), channel_id=1, source_target_pairs={{0,1},{1,0},{2,3},{3,2},{4,5},{5,4},{6,7},{7,6},{8,9},{9,8},{10,11... | collective-permute-start | bytes 589832 | tf_op jit(solution)/shard_map/ppermute | solution.py:341
  103.5 10.8 %collective-permute-start.23 = (bf16[256,384]{1,0:T(8,128)(2,1)S(1)}, bf16[256,384]{1,0:T(8,128)(2,1)S(1)}, u32[]{:S(2)}, u32[]{:S(2)}) collective-permute-start(bf16[256,384]{1,0:T(8,128)(2,1)S(1)} %get-tuple-element.89), channel_id=1, source_target_pairs={{0,3},{1,2},{2,1},{3,0},{4,7},{5,6},{6,5},{7,4},{8,11},{9,10},{10,... | collective-permute-start | bytes 589832 | tf_op jit(solution)/shard_map/ppermute | solution.py:344
  106.3 8.0 %collective-permute-start.21 = (bf16[256,384]{1,0:T(8,128)(2,1)S(1)}, bf16[256,384]{1,0:T(8,128)(2,1)S(1)}, u32[]{:S(2)}, u32[]{:S(2)}) collective-permute-start(bf16[256,384]{1,0:T(8,128)(2,1)S(1)} %get-tuple-element.89), channel_id=1, source_target_pairs={{0,2},{2,0},{4,6},{6,4},{8,10},{10,8},{12,14},{14,12},{16,18},{18,... | collective-permute-start | bytes 589832 | tf_op jit(solution)/shard_map/ppermute | solution.py:338
  116.0 16.6 %collective-permute-start.24 = (bf16[256,768]{1,0:T(8,128)(2,1)S(1)}, bf16[256,768]{1,0:T(8,128)(2,1)S(1)}, u32[]{:S(2)}, u32[]{:S(2)}) collective-permute-start(bf16[256,768]{1,0:T(8,128)(2,1)S(1)} %get-tuple-element.91), channel_id=1, source_target_pairs={{0,252},{2,254},{4,0},{6,2},{8,4},{10,6},{12,8},{14,10},{16,12},{1... | collective-permute-start | bytes 1179656 | tf_op jit(solution)/shard_map/ppermute | solution.py:338
  116.1 20.2 %collective-permute-start.25 = (bf16[256,768]{1,0:T(8,128)(2,1)S(1)}, bf16[256,768]{1,0:T(8,128)(2,1)S(1)}, u32[]{:S(2)}, u32[]{:S(2)}) collective-permute-start(bf16[256,768]{1,0:T(8,128)(2,1)S(1)} %get-tuple-element.93), channel_id=1, source_target_pairs={{0,254},{2,0},{4,2},{6,4},{8,6},{10,8},{12,10},{14,12},{16,14},{18... | collective-permute-start | bytes 1179656 | tf_op jit(solution)/shard_map/ppermute | solution.py:338
  (8 other events, 33.4 us)
where the time goes:
time: 139 us; the launch traced here: 138 us
  waiting for transfers between devices  73.7 us (53%)
  Pallas kernels  35.3 us (25%)
  starting transfers between devices  22.4 us (16%)
  local copies, waits for them, and re-layouts  5.6 us (4%)
    ppermute x14, waiting for transfers between devices, on_queue(): return lax.ppermute(x, 'queue', perm)  48 us
    pallas_call x11, Pallas kernels, call(): pl.pallas_call(body, grid_spec=pltpu.PrefetchScalarGridSpec(num_scalar_pr...  35.3 us
    ppermute x6, waiting for transfers between devices, on_both(): return lax.ppermute(x, both, perm)  23.4 us
    ppermute x6, starting transfers between devices, on_both(): return lax.ppermute(x, both, perm)  10.8 us
    ppermute x14, starting transfers between devices, on_queue(): return lax.ppermute(x, 'queue', perm)  8.94 us
    unnamed x28, local copies, waits for them, and re-layouts  5.49 us
  transfers between devices with their start and end apart: 26, of which 13 were waited for; matrix products, arithmetic and copies ran while one was open for 0% of the time, Pallas kernels for 15%

commit v1 on v0

--- a/solution.py
+++ b/solution.py
@@ -368,6 +368,7 @@
         functools.partial(prepare_body, queue), [meta, level_index],
         [jnp.transpose(w_mod, (1, 0, 2))], [None],
         [jax.ShapeDtypeStruct((TABLE_ROWS, half), F32)],
+        room=58 * 1024 * 1024,
     )
     mod_theirs = on_sides(mod_mine)
     w_query, w_pair, *send = call(

time: 139 us -> 139 us (level)
  local copies, waits for them, and re-layouts: 5.6 us -> 3.68 us
  Pallas kernels: 35.3 us -> 37.2 us
    unnamed x28 -> x24, local copies, waits for them, and re-layouts: 5.49 us -> 2.97 us
    pallas_call x11, Pallas kernels: 35.3 us -> 37.2 us  [call(): pl.pallas_call(body, grid_spec=pltpu.PrefetchScalarGridSpec(num_scalar_pr...]
  transfers between devices with their start and end apart: 26 -> 26, of which waited for: 13 -> 13; matrix products, arithmetic and copies ran while one was open for 0% -> 1% of each run, Pallas kernels for 15% -> 17%
where the time goes in v1:
time: 139 us; the launch traced here: 138 us
  waiting for transfers between devices  72.8 us (52%)
  Pallas kernels  37.2 us (27%)
  starting transfers between devices  23.3 us (17%)
  local copies, waits for them, and re-layouts  3.68 us (3%)
    ppermute x14, waiting for transfers between devices, on_queue(): return lax.ppermute(x, 'queue', perm)  47.7 us
    pallas_call x11, Pallas kernels, call(): pl.pallas_call(body, grid_spec=pltpu.PrefetchScalarGridSpec(num_scalar_pr...  37.2 us
    ppermute x6, waiting for transfers between devices, on_both(): return lax.ppermute(x, both, perm)  22.7 us
    ppermute x6, starting transfers between devices, on_both(): return lax.ppermute(x, both, perm)  11.4 us
    ppermute x14, starting transfers between devices, on_queue(): return lax.ppermute(x, 'queue', perm)  9.3 us
    unnamed x24, local copies, waits for them, and re-layouts  2.97 us
  transfers between devices with their start and end apart: 26, of which 13 were waited for; matrix products, arithmetic and copies ran while one was open for 1% of the time, Pallas kernels for 17%

profile of v1, /device:TPU:231, one launch (start us, length us, event | category | flops | bytes accessed | tf_op | source)
XLA Modules:
  0.0 137.8 jit_solution(12480384459391008308)
XLA Ops:
  0.6 1.4 %collective-permute-start.2 = (bf16[256,768]{1,0:T(8,128)(2,1)}, bf16[256,768]{1,0:T(8,128)(2,1)S(1)}, u32[]{:S(2)}, u32[]{:S(2)}) collective-permute-start(bf16[256,768]{1,0:T(8,128)(2,1)} %bitcast.13), channel_id=1, source_target_pairs={{0,1},{1,0},{2,3},{3,2},{4,5},{5,4},{6,7},{7,6},{8,9},{9,8},{10,11... | collective-permute-start | bytes 1179656 | tf_op jit(solution)/shard_map/ppermute | solution.py:341
  2.0 1.9 %collective-permute-start.1 = (bf16[256,768]{1,0:T(8,128)(2,1)}, bf16[256,768]{1,0:T(8,128)(2,1)S(1)}, u32[]{:S(2)}, u32[]{:S(2)}) collective-permute-start(bf16[256,768]{1,0:T(8,128)(2,1)} %bitcast.14), channel_id=1, source_target_pairs={{0,0},{1,1},{2,2},{3,3},{4,8},{5,9},{6,10},{7,11},{8,4},{9,5},{10,... | collective-permute-start | bytes 1179656 | tf_op jit(solution)/shard_map/ppermute | solution.py:344
  3.9 1.5 %collective-permute-start = (bf16[256,768]{1,0:T(8,128)(2,1)}, bf16[256,768]{1,0:T(8,128)(2,1)S(1)}, u32[]{:S(2)}, u32[]{:S(2)}) collective-permute-start(bf16[256,768]{1,0:T(8,128)(2,1)} %bitcast.15), channel_id=1, source_target_pairs={{0,4},{2,6},{4,0},{6,2},{8,12},{10,14},{12,8},{14,10},{16,20},{18,... | collective-permute-start | bytes 1179656 | tf_op jit(solution)/shard_map/ppermute | solution.py:338
  5.5 1.5 %collective-permute-start.6 = (bf16[256,768]{1,0:T(8,128)(2,1)}, bf16[256,768]{1,0:T(8,128)(2,1)S(1)}, u32[]{:S(2)}, u32[]{:S(2)}) collective-permute-start(bf16[256,768]{1,0:T(8,128)(2,1)} %bitcast.16), channel_id=1, source_target_pairs={{0,2},{2,0},{4,6},{6,4},{8,10},{10,8},{12,14},{14,12},{16,18},{18,... | collective-permute-start | bytes 1179656 | tf_op jit(solution)/shard_map/ppermute | solution.py:338
  7.7 2.9 %shard_map.104.mod_m.refs_4_.rest_16_.rest_8_ = f32[24,768]{1,0:T(8,128)} custom-call(s32[5]{0:T(128)} %stack.23.meta_ref, s32[128]{0:T(128)} %level_ref.1, bf16[3,256,768]{2,1,0:T(8,128)(2,1)} %bitcast.19), custom_call_target="tpu_custom_call" | custom-call | flops 1 | bytes 1 | tf_op jit(solution)/shard_map/pallas_call | solution.py:32
  10.8 5.6 %shard_map.105 = (bf16[1536,384]{1,0:T(8,128)(2,1)}, bf16[1536,768]{1,0:T(8,128)(2,1)}, bf16[256,1536]{1,0:T(8,128)(2,1)}, bf16[128,1536]{1,0:T(8,128)(2,1)}) custom-call(s32[5]{0:T(128)} %stack.23.meta_ref, bf16[1536,768]{1,0:T(8,128)(2,1)} %wq.1, bf16[1536,768]{1,0:T(8,128)(2,1)} %wk.1, bf16[1536,768]{1,0:T(8,128)(2,1)} %wv.1, bf16[768,1536]{1,0:T(8,128)(2,1)} %rest_1_.3), custom_call_target="tpu_custom_call" | custom-call | flops 1 | bytes 1 | tf_op jit(solution)/shard_map/pallas_call | solution.py:32
  16.4 2.8 %collective-permute-done.1.refs_2_ = bf16[256,768]{1,0:T(8,128)(2,1)S(1)} collective-permute-done((bf16[256,768]{1,0:T(8,128)(2,1)}, bf16[256,768]{1,0:T(8,128)(2,1)S(1)}, u32[]{:S(2)}, u32[]{:S(2)}) %collective-permute-start.1) | collective-permute-done | bytes 393248 | tf_op jit(solution)/shard_map/ppermute | solution.py:344
  19.2 1.9 %collective-permute-start.7 = (bf16[256,768]{1,0:T(8,128)(2,1)S(1)}, bf16[256,768]{1,0:T(8,128)(2,1)S(1)}, u32[]{:S(2)}, u32[]{:S(2)}) collective-permute-start(bf16[256,768]{1,0:T(8,128)(2,1)S(1)} %collective-permute-done.2.own_t.rest_13_), channel_id=1, source_target_pairs={{0,2},{2,0},{4,6},{6,4},{8,10},{10,8},{12,14},{14,12},{16,18},{18,... | collective-permute-start | bytes 1179656 | tf_op jit(solution)/shard_map/ppermute | solution.py:338
  22.0 4.1 %collective-permute-start.4 = (bf16[256,768]{1,0:T(8,128)(2,1)S(1)}, bf16[256,768]{1,0:T(8,128)(2,1)S(1)}, u32[]{:S(2)}, u32[]{:S(2)}) collective-permute-start(bf16[256,768]{1,0:T(8,128)(2,1)S(1)} %collective-permute-done.2.own_t.rest_13_), channel_id=1, source_target_pairs={{0,0},{1,1},{2,2},{3,3},{4,8},{5,9},{6,10},{7,11},{8,4},{9,5},{10,... | collective-permute-start | bytes 1179656 | tf_op jit(solution)/shard_map/ppermute | solution.py:344
  26.2 1.7 %copy-done.1 = bf16[1536,768]{1,0:T(8,128)(2,1)S(1)} copy-done((bf16[1536,768]{1,0:T(8,128)(2,1)S(1)}, bf16[1536,768]{1,0:T(8,128)(2,1)}, u32[]{:S(2)}) %copy-start.1) | copy-done | bytes 2359320
  29.1 5.8 %shard_map.106 = (bf16[2,256,384]{2,1,0:T(8,128)(2,1)S(1)}, f32[2,256,384]{2,1,0:T(8,128)S(1)}, f32[2,256,128]{2,1,0:T(8,128)S(1)}) custom-call(s32[5]{0:T(128)S(1)} %copy-done.8, s32[128]{0:T(128)S(1)} %copy-done.9, bf16[256,768]{1,0:T(8,128)(2,1)S(1)} %bitcast.17, bf16[256,768]{1,0:T(8,128)(2,1)S(1)} %collective-permute-done.2.own_t.rest_13_, ...), custom_call_target="tpu_custom_call" | custom-call | flops 1 | bytes 1 | tf_op jit(solution)/shard_map/pallas_call | solution.py:32
  35.0 5.1 %collective-permute-done.4.refs_3_ = bf16[256,768]{1,0:T(8,128)(2,1)S(1)} collective-permute-done((bf16[256,768]{1,0:T(8,128)(2,1)S(1)}, bf16[256,768]{1,0:T(8,128)(2,1)S(1)}, u32[]{:S(2)}, u32[]{:S(2)}) %collective-permute-start.4) | collective-permute-done | bytes 393248 | tf_op jit(solution)/shard_map/ppermute | solution.py:344
  40.1 1.6 %shard_map.107 = (bf16[256,1536]{1,0:T(8,128)(2,1)S(1)}, bf16[256,1536]{1,0:T(8,128)(2,1)S(1)}) custom-call(s32[5]{0:T(128)S(1)} %copy-done.8, bf16[256,768]{1,0:T(8,128)(2,1)S(1)} %collective-permute-done.refs_0_, bf16[256,768]{1,0:T(8,128)(2,1)S(1)} %collective-permute-done.3.refs_1_, bf16[256,768]{1,0:T(8,128)(2,1)S(1)} %collective-permute-done.1.refs_2_, ...), custom_call_target="tpu_custom_call" | custom-call | flops 1 | bytes 1 | tf_op jit(solution)/shard_map/pallas_call | solution.py:32
  43.3 1.3 collective-permute-done.9.refs_1_
  45.7 6.0 %shard_map.108 = (bf16[256,384]{1,0:T(8,128)(2,1)S(1)}, bf16[256,384]{1,0:T(8,128)(2,1)S(1)}) custom-call(s32[5]{0:T(128)S(1)} %copy-done.8, s32[128]{0:T(128)S(1)} %copy-done.9, bf16[256,1536]{1,0:T(8,128)(2,1)S(1)} %get-tuple-element.71.refs_0_, bf16[256,1536]{1,0:T(8,128)(2,1)S(1)} %collective-permute-done.9.refs_1_, ...), custom_call_target="tpu_custom_call" | custom-call | flops 1 | bytes 1 | tf_op jit(solution)/shard_map/pallas_call | solution.py:32
  52.0 1.8 %collective-permute-start.13 = (bf16[256,384]{1,0:T(8,128)(2,1)S(1)}, bf16[256,384]{1,0:T(8,128)(2,1)S(1)}, u32[]{:S(2)}, u32[]{:S(2)}) collective-permute-start(bf16[256,384]{1,0:T(8,128)(2,1)S(1)} %get-tuple-element.77), channel_id=1, source_target_pairs={{0,3},{1,2},{2,1},{3,0},{4,7},{5,6},{6,5},{7,4},{8,11},{9,10},{10,... | collective-permute-start | bytes 589832 | tf_op jit(solution)/shard_map/ppermute | solution.py:344
  53.8 8.8 %collective-permute-done.14.rest_2_.rest_8_ = bf16[256,1536]{1,0:T(8,128)(2,1)S(1)} collective-permute-done((bf16[256,1536]{1,0:T(8,128)(2,1)S(1)}, bf16[256,1536]{1,0:T(8,128)(2,1)S(1)}, u32[]{:S(2)}, u32[]{:S(2)}) %collective-permute-start.14) | collective-permute-done | bytes 786464 | tf_op jit(solution)/shard_map/ppermute | solution.py:344
  64.4 2.2 %collective-permute-done.11.m_core = bf16[256,384]{1,0:T(8,128)(2,1)S(1)} collective-permute-done((bf16[256,384]{1,0:T(8,128)(2,1)S(1)}, bf16[256,384]{1,0:T(8,128)(2,1)S(1)}, u32[]{:S(2)}, u32[]{:S(2)}) %collective-permute-start.11) | collective-permute-done | bytes 196640 | tf_op jit(solution)/shard_map/ppermute | solution.py:338
  66.7 3.1 %shard_map.109 = (bf16[256,768]{1,0:T(8,128)(2,1)S(1)}, bf16[256,768]{1,0:T(8,128)(2,1)S(1)}, bf16[256,1536]{1,0:T(8,128)(2,1)S(1)}) custom-call(s32[5]{0:T(128)S(1)} %copy-done.8, bf16[256,384]{1,0:T(8,128)(2,1)S(1)} %get-tuple-element.76.m_self, bf16[256,384]{1,0:T(8,128)(2,1)S(1)} %collective-permute-done.11.m_core, ...), custom_call_target="tpu_custom_call" | custom-call | flops 1 | bytes 1 | tf_op jit(solution)/shard_map/pallas_call | solution.py:32
  70.2 1.9 %collective-permute-done.18.other = bf16[256,1536]{1,0:T(8,128)(2,1)S(1)} collective-permute-done((bf16[256,1536]{1,0:T(8,128)(2,1)S(1)}, bf16[256,1536]{1,0:T(8,128)(2,1)S(1)}, u32[]{:S(2)}, u32[]{:S(2)}) %collective-permute-start.18) | collective-permute-done | bytes 786464 | tf_op jit(solution)/shard_map/ppermute | solution.py:338
  72.1 2.7 %shard_map.110 = (bf16[2,256,384]{2,1,0:T(8,128)(2,1)S(1)}, bf16[2,256,768]{2,1,0:T(8,128)(2,1)S(1)}) custom-call(s32[5]{0:T(128)S(1)} %copy-done.8, bf16[256,1536]{1,0:T(8,128)(2,1)S(1)} %get-tuple-element.83.own, bf16[256,1536]{1,0:T(8,128)(2,1)S(1)} %collective-permute-done.18.other, bf16[1536,384]{1,0:T(8,128)(2,1)S(1)} %copy-done.5, ...), custom_call_target="tpu_custom_call" | custom-call | flops 1 | bytes 1 | tf_op jit(solution)/shard_map/pallas_call | solution.py:32
  74.9 1.3 collective-permute-start.20
  76.2 2.5 %shard_map.111 = (f32[2,256,384]{2,1,0:T(8,128)S(1)}, f32[2,256,128]{2,1,0:T(8,128)S(1)}) custom-call(s32[5]{0:T(128)S(1)} %copy-done.8, s32[128]{0:T(128)S(1)} %copy-done.9, bf16[2,256,384]{2,1,0:T(8,128)(2,1)S(1)} %get-tuple-element.85.q_ref.refs_2_, bf16[2,256,768]{2,1,0:T(8,128)(2,1)S(1)} %get-tuple-element.84.kv_ref), custom_call_target="tpu_custom_call" | custom-call | flops 1 | bytes 1 | tf_op jit(solution)/shard_map/pallas_call | solution.py:32
  78.7 21.0 %collective-permute-done.20.refs_1_ = bf16[2,256,768]{2,1,0:T(8,128)(2,1)S(1)} collective-permute-done((bf16[2,256,768]{2,1,0:T(8,128)(2,1)S(1)}, bf16[2,256,768]{2,1,0:T(8,128)(2,1)S(1)}, u32[]{:S(2)}, u32[]{:S(2)}) %collective-permute-start.20) | collective-permute-done | bytes 786464 | tf_op jit(solution)/shard_map/ppermute | solution.py:338
  99.7 3.7 %shard_map.112 = (bf16[256,384]{1,0:T(8,128)(2,1)S(1)}, bf16[256,384]{1,0:T(8,128)(2,1)S(1)}) custom-call(s32[5]{0:T(128)S(1)} %copy-done.8, s32[128]{0:T(128)S(1)} %copy-done.9, bf16[2,256,768]{2,1,0:T(8,128)(2,1)S(1)} %collective-permute-done.19.refs_0_, bf16[2,256,768]{2,1,0:T(8,128)(2,1)S(1)} %collective-permute-done.20.refs_1_, ...), custom_call_target="tpu_custom_call" | custom-call | flops 1 | bytes 1 | tf_op jit(solution)/shard_map/pallas_call | solution.py:32
  103.5 2.8 %collective-permute-start.23 = (bf16[256,384]{1,0:T(8,128)(2,1)S(1)}, bf16[256,384]{1,0:T(8,128)(2,1)S(1)}, u32[]{:S(2)}, u32[]{:S(2)}) collective-permute-start(bf16[256,384]{1,0:T(8,128)(2,1)S(1)} %get-tuple-element.89), channel_id=1, source_target_pairs={{0,3},{1,2},{2,1},{3,0},{4,7},{5,6},{6,5},{7,4},{8,11},{9,10},{10,... | collective-permute-start | bytes 589832 | tf_op jit(solution)/shard_map/ppermute | solution.py:344
  106.3 2.3 %collective-permute-done.22.m_y = bf16[256,384]{1,0:T(8,128)(2,1)S(1)} collective-permute-done((bf16[256,384]{1,0:T(8,128)(2,1)S(1)}, bf16[256,384]{1,0:T(8,128)(2,1)S(1)}, u32[]{:S(2)}, u32[]{:S(2)}) %collective-permute-start.22) | collective-permute-done | bytes 196640 | tf_op jit(solution)/shard_map/ppermute | solution.py:341
  108.6 5.7 %collective-permute-done.23.m_yx = bf16[256,384]{1,0:T(8,128)(2,1)S(1)} collective-permute-done((bf16[256,384]{1,0:T(8,128)(2,1)S(1)}, bf16[256,384]{1,0:T(8,128)(2,1)S(1)}, u32[]{:S(2)}, u32[]{:S(2)}) %collective-permute-start.23) | collective-permute-done | bytes 196640 | tf_op jit(solution)/shard_map/ppermute | solution.py:344
  114.3 1.6 %shard_map.113 = (bf16[256,768]{1,0:T(8,128)(2,1)S(1)}, bf16[256,768]{1,0:T(8,128)(2,1)S(1)}) custom-call(s32[5]{0:T(128)S(1)} %copy-done.8, bf16[256,384]{1,0:T(8,128)(2,1)S(1)} %get-tuple-element.88.m_self, bf16[256,384]{1,0:T(8,128)(2,1)S(1)} %collective-permute-done.21.m_core, bf16[256,384]{1,0:T(8,128)(2,1)S(1)} %collective-permute-done.22.m_y, ...), custom_call_target="tpu_custom_call" | custom-call | flops 1 | bytes 1 | tf_op jit(solution)/shard_map/pallas_call | solution.py:32
  116.1 16.4 %collective-permute-done.24.latent = bf16[256,768]{1,0:T(8,128)(2,1)S(1)} collective-permute-done((bf16[256,768]{1,0:T(8,128)(2,1)S(1)}, bf16[256,768]{1,0:T(8,128)(2,1)S(1)}, u32[]{:S(2)}, u32[]{:S(2)}) %collective-permute-start.24) | collective-permute-done | bytes 393248 | tf_op jit(solution)/shard_map/ppermute | solution.py:338
  132.5 3.7 %collective-permute-done.25.second = bf16[256,768]{1,0:T(8,128)(2,1)S(1)} collective-permute-done((bf16[256,768]{1,0:T(8,128)(2,1)S(1)}, bf16[256,768]{1,0:T(8,128)(2,1)S(1)}, u32[]{:S(2)}, u32[]{:S(2)}) %collective-permute-start.25) | collective-permute-done | bytes 393248 | tf_op jit(solution)/shard_map/ppermute | solution.py:338
  136.2 1.6 %shard_map.114 = (bf16[256,768]{1,0:T(8,128)(2,1)}, bf16[2,256,768]{2,1,0:T(8,128)(2,1)}) custom-call(s32[5]{0:T(128)S(1)} %copy-done.8, bf16[256,768]{1,0:T(8,128)(2,1)S(1)} %collective-permute-done.24.latent, bf16[256,768]{1,0:T(8,128)(2,1)S(1)} %get-tuple-element.92.first, bf16[256,768]{1,0:T(8,128)(2,1)S(1)} %collective-permute-done.25.second), custom_call_target="tpu_custom_call" | custom-call | flops 1 | bytes 1 | tf_op jit(solution)/shard_map/pallas_call | solution.py:32
  (57 shorter events, 8.6 us)
Async XLA Ops:
  0.6 15.8 %collective-permute-start.2 = (bf16[256,768]{1,0:T(8,128)(2,1)}, bf16[256,768]{1,0:T(8,128)(2,1)S(1)}, u32[]{:S(2)}, u32[]{:S(2)}) collective-permute-start(bf16[256,768]{1,0:T(8,128)(2,1)} %bitcast.13), channel_id=1, source_target_pairs={{0,1},{1,0},{2,3},{3,2},{4,5},{5,4},{6,7},{7,6},{8,9},{9,8},{10,11... | collective-permute-start | bytes 1179656 | tf_op jit(solution)/shard_map/ppermute | solution.py:341
  2.0 17.2 %collective-permute-start.1 = (bf16[256,768]{1,0:T(8,128)(2,1)}, bf16[256,768]{1,0:T(8,128)(2,1)S(1)}, u32[]{:S(2)}, u32[]{:S(2)}) collective-permute-start(bf16[256,768]{1,0:T(8,128)(2,1)} %bitcast.14), channel_id=1, source_target_pairs={{0,0},{1,1},{2,2},{3,3},{4,8},{5,9},{6,10},{7,11},{8,4},{9,5},{10,... | collective-permute-start | bytes 1179656 | tf_op jit(solution)/shard_map/ppermute | solution.py:344
  3.9 15.3 %collective-permute-start = (bf16[256,768]{1,0:T(8,128)(2,1)}, bf16[256,768]{1,0:T(8,128)(2,1)S(1)}, u32[]{:S(2)}, u32[]{:S(2)}) collective-permute-start(bf16[256,768]{1,0:T(8,128)(2,1)} %bitcast.15), channel_id=1, source_target_pairs={{0,4},{2,6},{4,0},{6,2},{8,12},{10,14},{12,8},{14,10},{16,20},{18,... | collective-permute-start | bytes 1179656 | tf_op jit(solution)/shard_map/ppermute | solution.py:338
  5.5 20.6 %collective-permute-start.6 = (bf16[256,768]{1,0:T(8,128)(2,1)}, bf16[256,768]{1,0:T(8,128)(2,1)S(1)}, u32[]{:S(2)}, u32[]{:S(2)}) collective-permute-start(bf16[256,768]{1,0:T(8,128)(2,1)} %bitcast.16), channel_id=1, source_target_pairs={{0,2},{2,0},{4,6},{6,4},{8,10},{10,8},{12,14},{14,12},{16,18},{18,... | collective-permute-start | bytes 1179656 | tf_op jit(solution)/shard_map/ppermute | solution.py:338
  10.5 15.6 %copy-start.8 = (s32[5]{0:T(128)S(1)}, s32[5]{0:T(128)}, u32[]{:S(2)}) copy-start(s32[5]{0:T(128)} %stack.23.meta_ref) | copy-start | bytes 64
  10.5 15.6 %copy-start.9 = (s32[128]{0:T(128)S(1)}, s32[128]{0:T(128)}, u32[]{:S(2)}) copy-start(s32[128]{0:T(128)} %width_ref.7) | copy-start | bytes 1540
  10.6 11.5 %collective-permute-start.8 = (f32[24,768]{1,0:T(8,128)}, f32[24,768]{1,0:T(8,128)S(1)}, u32[]{:S(2)}, u32[]{:S(2)}) collective-permute-start(f32[24,768]{1,0:T(8,128)} %shard_map.104.mod_m.refs_4_.rest_16_.rest_8_), channel_id=1, source_target_pairs={{0,1},{1,0},{2,3},{3,2},{4,5},{5,4},{6,7},{7,6},{8,9},{9,8},{10,11... | collective-permute-start | bytes 221192 | tf_op jit(solution)/shard_map/ppermute | solution.py:341
  19.2 6.9 %collective-permute-start.7 = (bf16[256,768]{1,0:T(8,128)(2,1)S(1)}, bf16[256,768]{1,0:T(8,128)(2,1)S(1)}, u32[]{:S(2)}, u32[]{:S(2)}) collective-permute-start(bf16[256,768]{1,0:T(8,128)(2,1)S(1)} %collective-permute-done.2.own_t.rest_13_), channel_id=1, source_target_pairs={{0,2},{2,0},{4,6},{6,4},{8,10},{10,8},{12,14},{14,12},{16,18},{18,... | collective-permute-start | bytes 1179656 | tf_op jit(solution)/shard_map/ppermute | solution.py:338
  21.1 21.7 %copy-start.10 = (bf16[256,1536]{1,0:T(8,128)(2,1)S(1)}, bf16[256,1536]{1,0:T(8,128)(2,1)}, u32[]{:S(2)}) copy-start(bf16[256,1536]{1,0:T(8,128)(2,1)} %get-tuple-element.78) | copy-start | bytes 2359300
  21.1 13.8 %collective-permute-start.5 = (bf16[256,768]{1,0:T(8,128)(2,1)S(1)}, bf16[256,768]{1,0:T(8,128)(2,1)S(1)}, u32[]{:S(2)}, u32[]{:S(2)}) collective-permute-start(bf16[256,768]{1,0:T(8,128)(2,1)S(1)} %slice_bitcast_fusion), channel_id=1, source_target_pairs={{0,1},{1,0},{2,2},{3,3},{4,4},{5,5},{6,6},{7,7},{8,8},{9,9},{10,10... | collective-permute-start | bytes 1179656 | tf_op jit(solution)/shard_map/ppermute | solution.py:344
  21.9 13.0 %collective-permute-start.3 = (bf16[256,768]{1,0:T(8,128)(2,1)S(1)}, bf16[256,768]{1,0:T(8,128)(2,1)S(1)}, u32[]{:S(2)}, u32[]{:S(2)}) collective-permute-start(bf16[256,768]{1,0:T(8,128)(2,1)S(1)} %collective-permute-done.refs_0_), channel_id=1, source_target_pairs={{0,1},{1,0},{2,3},{3,2},{4,5},{5,4},{6,7},{7,6},{8,9},{9,8},{10,11... | collective-permute-start | bytes 1179656 | tf_op jit(solution)/shard_map/ppermute | solution.py:341
  22.0 18.1 %collective-permute-start.4 = (bf16[256,768]{1,0:T(8,128)(2,1)S(1)}, bf16[256,768]{1,0:T(8,128)(2,1)S(1)}, u32[]{:S(2)}, u32[]{:S(2)}) collective-permute-start(bf16[256,768]{1,0:T(8,128)(2,1)S(1)} %collective-permute-done.2.own_t.rest_13_), channel_id=1, source_target_pairs={{0,0},{1,1},{2,2},{3,3},{4,8},{5,9},{6,10},{7,11},{8,4},{9,5},{10,... | collective-permute-start | bytes 1179656 | tf_op jit(solution)/shard_map/ppermute | solution.py:344
  29.1 16.6 %copy-start.2 = (bf16[1536,768]{1,0:T(8,128)(2,1)S(1)}, bf16[1536,768]{1,0:T(8,128)(2,1)}, u32[]{:S(2)}) copy-start(bf16[1536,768]{1,0:T(8,128)(2,1)} %get-tuple-element.55.wkv.refs_4_) | copy-start | bytes 7077892
  41.7 24.9 %copy-start = (bf16[768,1536]{1,0:T(8,128)(2,1)S(1)}, bf16[768,1536]{1,0:T(8,128)(2,1)}, u32[]{:S(2)}) copy-start(bf16[768,1536]{1,0:T(8,128)(2,1)} %rest_1_.3) | copy-start | bytes 7077892
  41.8 2.8 %collective-permute-start.9 = (bf16[256,1536]{1,0:T(8,128)(2,1)S(1)}, bf16[256,1536]{1,0:T(8,128)(2,1)S(1)}, u32[]{:S(2)}, u32[]{:S(2)}) collective-permute-start(bf16[256,1536]{1,0:T(8,128)(2,1)S(1)} %get-tuple-element.71.refs_0_), channel_id=1, source_target_pairs={{0,2},{2,0},{4,6},{6,4},{8,10},{10,8},{12,14},{14,12},{16,18},{18,... | collective-permute-start | bytes 2359304 | tf_op jit(solution)/shard_map/ppermute | solution.py:338
  42.6 3.0 %collective-permute-start.10 = (bf16[256,1536]{1,0:T(8,128)(2,1)S(1)}, bf16[256,1536]{1,0:T(8,128)(2,1)S(1)}, u32[]{:S(2)}, u32[]{:S(2)}) collective-permute-start(bf16[256,1536]{1,0:T(8,128)(2,1)S(1)} %get-tuple-element.72.refs_2_), channel_id=1, source_target_pairs={{0,2},{2,0},{4,6},{6,4},{8,10},{10,8},{12,14},{14,12},{16,18},{18,... | collective-permute-start | bytes 2359304 | tf_op jit(solution)/shard_map/ppermute | solution.py:338
  42.8 19.9 %collective-permute-start.14 = (bf16[256,1536]{1,0:T(8,128)(2,1)S(1)}, bf16[256,1536]{1,0:T(8,128)(2,1)S(1)}, u32[]{:S(2)}, u32[]{:S(2)}) collective-permute-start(bf16[256,1536]{1,0:T(8,128)(2,1)S(1)} %copy-done.10), channel_id=1, source_target_pairs={{0,129},{1,128},{2,131},{3,130},{4,133},{5,132},{6,135},{7,134},{8... | collective-permute-start | bytes 2359304 | tf_op jit(solution)/shard_map/ppermute | solution.py:344
  42.8 11.1 %collective-permute-start.15 = (bf16[128,1536]{1,0:T(8,128)(2,1)S(1)}, bf16[128,1536]{1,0:T(8,128)(2,1)S(1)}, u32[]{:S(2)}, u32[]{:S(2)}) collective-permute-start(bf16[128,1536]{1,0:T(8,128)(2,1)S(1)} %copy-done.11), channel_id=1, source_target_pairs={{0,1},{1,0},{2,3},{3,2},{4,5},{5,4},{6,7},{7,6},{8,9},{9,8},{10,11... | collective-permute-start | bytes 1179656 | tf_op jit(solution)/shard_map/ppermute | solution.py:341
  51.7 10.9 %collective-permute-start.12 = (bf16[256,384]{1,0:T(8,128)(2,1)S(1)}, bf16[256,384]{1,0:T(8,128)(2,1)S(1)}, u32[]{:S(2)}, u32[]{:S(2)}) collective-permute-start(bf16[256,384]{1,0:T(8,128)(2,1)S(1)} %get-tuple-element.76.m_self), channel_id=1, source_target_pairs={{0,1},{1,0},{2,3},{3,2},{4,5},{5,4},{6,7},{7,6},{8,9},{9,8},{10,11... | collective-permute-start | bytes 589832 | tf_op jit(solution)/shard_map/ppermute | solution.py:341
  52.0 20.1 %copy-start.5 = (bf16[1536,384]{1,0:T(8,128)(2,1)S(1)}, bf16[1536,384]{1,0:T(8,128)(2,1)}, u32[]{:S(2)}) copy-start(bf16[1536,384]{1,0:T(8,128)(2,1)} %get-tuple-element.54.wq) | copy-start | bytes 3538948
  52.0 10.9 %collective-permute-start.13 = (bf16[256,384]{1,0:T(8,128)(2,1)S(1)}, bf16[256,384]{1,0:T(8,128)(2,1)S(1)}, u32[]{:S(2)}, u32[]{:S(2)}) collective-permute-start(bf16[256,384]{1,0:T(8,128)(2,1)S(1)} %get-tuple-element.77), channel_id=1, source_target_pairs={{0,3},{1,2},{2,1},{3,0},{4,7},{5,6},{6,5},{7,4},{8,11},{9,10},{10,... | collective-permute-start | bytes 589832 | tf_op jit(solution)/shard_map/ppermute | solution.py:344
  63.0 3.7 %collective-permute-start.16 = (bf16[256,1536]{1,0:T(8,128)(2,1)S(1)}, bf16[256,1536]{1,0:T(8,128)(2,1)S(1)}, u32[]{:S(2)}, u32[]{:S(2)}) collective-permute-start(bf16[256,1536]{1,0:T(8,128)(2,1)S(1)} %collective-permute-done.14.rest_2_.rest_8_), channel_id=1, source_target_pairs={{0,2},{2,0},{4,6},{6,4},{8,10},{10,8},{12,14},{14,12},{16,18},{18,... | collective-permute-start | bytes 2359304 | tf_op jit(solution)/shard_map/ppermute | solution.py:338
  63.9 2.8 %collective-permute-start.17 = (bf16[128,1536]{1,0:T(8,128)(2,1)S(1)}, bf16[128,1536]{1,0:T(8,128)(2,1)S(1)}, u32[]{:S(2)}, u32[]{:S(2)}) collective-permute-start(bf16[128,1536]{1,0:T(8,128)(2,1)S(1)} %collective-permute-done.15.rest_3_.rest_9_), channel_id=1, source_target_pairs={{0,2},{2,0},{4,6},{6,4},{8,10},{10,8},{12,14},{14,12},{16,18},{18,... | collective-permute-start | bytes 1179656 | tf_op jit(solution)/shard_map/ppermute | solution.py:338
  64.0 2.7 %collective-permute-start.11 = (bf16[256,384]{1,0:T(8,128)(2,1)S(1)}, bf16[256,384]{1,0:T(8,128)(2,1)S(1)}, u32[]{:S(2)}, u32[]{:S(2)}) collective-permute-start(bf16[256,384]{1,0:T(8,128)(2,1)S(1)} %get-tuple-element.77), channel_id=1, source_target_pairs={{0,2},{2,0},{4,6},{6,4},{8,10},{10,8},{12,14},{14,12},{16,18},{18,... | collective-permute-start | bytes 589832 | tf_op jit(solution)/shard_map/ppermute | solution.py:338
  69.8 2.4 %collective-permute-start.18 = (bf16[256,1536]{1,0:T(8,128)(2,1)S(1)}, bf16[256,1536]{1,0:T(8,128)(2,1)S(1)}, u32[]{:S(2)}, u32[]{:S(2)}) collective-permute-start(bf16[256,1536]{1,0:T(8,128)(2,1)S(1)} %get-tuple-element.83.own), channel_id=1, source_target_pairs={{0,2},{2,0},{4,6},{6,4},{8,10},{10,8},{12,14},{14,12},{16,18},{18,... | collective-permute-start | bytes 2359304 | tf_op jit(solution)/shard_map/ppermute | solution.py:338
  74.9 24.8 %collective-permute-start.20 = (bf16[2,256,768]{2,1,0:T(8,128)(2,1)S(1)}, bf16[2,256,768]{2,1,0:T(8,128)(2,1)S(1)}, u32[]{:S(2)}, u32[]{:S(2)}) collective-permute-start(bf16[2,256,768]{2,1,0:T(8,128)(2,1)S(1)} %get-tuple-element.84.kv_ref), channel_id=1, source_target_pairs={{0,252},{2,254},{4,8},{6,10},{8,4},{10,6},{12,16},{14,18},{16,12},... | collective-permute-start | bytes 2359304 | tf_op jit(solution)/shard_map/ppermute | solution.py:338
  76.2 23.5 %collective-permute-start.19 = (bf16[2,256,768]{2,1,0:T(8,128)(2,1)S(1)}, bf16[2,256,768]{2,1,0:T(8,128)(2,1)S(1)}, u32[]{:S(2)}, u32[]{:S(2)}) collective-permute-start(bf16[2,256,768]{2,1,0:T(8,128)(2,1)S(1)} %get-tuple-element.84.kv_ref), channel_id=1, source_target_pairs={{0,4},{2,6},{4,0},{6,2},{8,12},{10,14},{12,8},{14,10},{16,20},{18,... | collective-permute-start | bytes 2359304 | tf_op jit(solution)/shard_map/ppermute | solution.py:338
  103.4 5.3 %collective-permute-start.22 = (bf16[256,384]{1,0:T(8,128)(2,1)S(1)}, bf16[256,384]{1,0:T(8,128)(2,1)S(1)}, u32[]{:S(2)}, u32[]{:S(2)}) collective-permute-start(bf16[256,384]{1,0:T(8,128)(2,1)S(1)} %get-tuple-element.88.m_self), channel_id=1, source_target_pairs={{0,1},{1,0},{2,3},{3,2},{4,5},{5,4},{6,7},{7,6},{8,9},{9,8},{10,11... | collective-permute-start | bytes 589832 | tf_op jit(solution)/shard_map/ppermute | solution.py:341
  103.5 10.8 %collective-permute-start.23 = (bf16[256,384]{1,0:T(8,128)(2,1)S(1)}, bf16[256,384]{1,0:T(8,128)(2,1)S(1)}, u32[]{:S(2)}, u32[]{:S(2)}) collective-permute-start(bf16[256,384]{1,0:T(8,128)(2,1)S(1)} %get-tuple-element.89), channel_id=1, source_target_pairs={{0,3},{1,2},{2,1},{3,0},{4,7},{5,6},{6,5},{7,4},{8,11},{9,10},{10,... | collective-permute-start | bytes 589832 | tf_op jit(solution)/shard_map/ppermute | solution.py:344
  106.3 8.0 %collective-permute-start.21 = (bf16[256,384]{1,0:T(8,128)(2,1)S(1)}, bf16[256,384]{1,0:T(8,128)(2,1)S(1)}, u32[]{:S(2)}, u32[]{:S(2)}) collective-permute-start(bf16[256,384]{1,0:T(8,128)(2,1)S(1)} %get-tuple-element.89), channel_id=1, source_target_pairs={{0,2},{2,0},{4,6},{6,4},{8,10},{10,8},{12,14},{14,12},{16,18},{18,... | collective-permute-start | bytes 589832 | tf_op jit(solution)/shard_map/ppermute | solution.py:338
  115.9 16.6 %collective-permute-start.24 = (bf16[256,768]{1,0:T(8,128)(2,1)S(1)}, bf16[256,768]{1,0:T(8,128)(2,1)S(1)}, u32[]{:S(2)}, u32[]{:S(2)}) collective-permute-start(bf16[256,768]{1,0:T(8,128)(2,1)S(1)} %get-tuple-element.91), channel_id=1, source_target_pairs={{0,252},{2,254},{4,0},{6,2},{8,4},{10,6},{12,8},{14,10},{16,12},{1... | collective-permute-start | bytes 1179656 | tf_op jit(solution)/shard_map/ppermute | solution.py:338
  116.0 20.2 %collective-permute-start.25 = (bf16[256,768]{1,0:T(8,128)(2,1)S(1)}, bf16[256,768]{1,0:T(8,128)(2,1)S(1)}, u32[]{:S(2)}, u32[]{:S(2)}) collective-permute-start(bf16[256,768]{1,0:T(8,128)(2,1)S(1)} %get-tuple-element.93), channel_id=1, source_target_pairs={{0,254},{2,0},{4,2},{6,4},{8,6},{10,8},{12,10},{14,12},{16,14},{18... | collective-permute-start | bytes 1179656 | tf_op jit(solution)/shard_map/ppermute | solution.py:338
  (6 other events, 58.3 us)
